TPU v7x, 256 devices: a whole 4x4x8 slice. The times are simulated.
256 devices in a mesh: seg: 16 (over y, x), sec: 16 (over z, core).
Axes of the slice: x: 4, y: 4, z: 8, core: 2. Of those that a mesh axis runs over, the one named last changes fastest.
Arguments:
- left_env: bfloat16 [16, 400, 256, 256], P('seg', 'sec'), as said below
- right_env: bfloat16 [16, 400, 256, 256], P('seg', 'sec'), as said below
- edge_site: bfloat16 [16, 256, 256], P('seg'), may hold values from -0.375 to 0.375
- psi_one: bfloat16 [16, 256, 256], P('seg'), may hold values from -6 to 6
- psi_two: bfloat16 [16, 256, 256], P('seg'), may hold values from -6 to 6
- mpo_gain: float32 [16, 400], P('seg', 'sec'), may hold values from 0.5 to 2
- kept: int32 [16, 2], P('seg'), may hold values from 64 to 256, as said below
Outputs:
- psi_first: float32 [16, 256, 256], P('seg', 'sec')
- psi_second: float32 [16, 256, 256], P('seg', 'sec')
Inputs may be any that keep to these rules, and one draw needn't show every extreme that they name: `kept`: some entry equals 256 and some equals 64. `left_env`: every [256, 256] block is symmetric, with entries of order (26214400) ** -0.25. `right_env`: every [256, 256] block is symmetric, with entries of order (26214400) ** -0.25.
All inputs are finite; a program needn't handle non-finite values.
Results may differ from a plain program's by a relative error of at most 0.03.
Values may be sent and summed in bfloat16 or wider, within the bound.
No kernel may reach another device: no remote copies, remote signals or barrier semaphores. Data moves between devices by JAX's collectives and lax.ppermute only.
A program may use at most 64 MiB of HBM per device.

v0:
```python
import jax
import jax.numpy as jnp
from jax import lax
from jax.sharding import PartitionSpec as P

ITERS = 3


epsilon = 1e-06
descent = 0.3


def shifted(value, axis, steps):
    count = lax.axis_size(axis)
    first, last = (max(0, -steps), min(count, count - steps))
    return lax.ppermute(value, axis, [(source, source + steps) for source in range(first, last)])


def apply_block(left_block, right_block, vector_bf):
    mpo_terms = left_block.shape[0]
    states = left_block.shape[1]
    partial_prod = jnp.dot(
        left_block.reshape(mpo_terms * states, states),
        vector_bf,
        preferred_element_type=jnp.float32,
    )
    partial_prod = partial_prod.astype(jnp.bfloat16).reshape(mpo_terms, states, states)
    return lax.dot_general(
        partial_prod, right_block, (((0, 2), (0, 2)), ((), ())), preferred_element_type=jnp.float32
    )


def rescale(vector, norm_sq, states):
    return states * vector / jnp.sqrt(norm_sq + epsilon)


def relax_block(left_block, right_block, start, live):
    states = start.shape[0]
    row_share = states // lax.axis_size("sec")
    row_start = lax.axis_index("sec") * row_share
    live_mask = (jnp.arange(states) < live).astype(jnp.float32)[:, None]
    initial = start.astype(jnp.float32) * live_mask
    vector = rescale(initial, jnp.sum(initial * initial), states)
    for sweep_step in range(ITERS):
        product = (
            lax.psum(
                apply_block(left_block, right_block, vector.astype(jnp.bfloat16)).astype(
                    jnp.bfloat16
                ),
                "sec",
            ).astype(jnp.float32)
            * live_mask
        )
        energy = jnp.sum(vector * product) / jnp.sum(vector * vector)
        stepped = vector - descent * (product - energy * vector)
        vector = rescale(stepped, jnp.sum(stepped * stepped), states)
    own_rows = lax.dynamic_slice_in_dim(vector, row_start, row_share, 0)
    return (own_rows, vector)


def on_device(left_env, right_env, edge_site, psi_one, psi_two, mpo_gain, kept):
    left_block = left_env[0]
    right_block = right_env[0]
    gain_row = mpo_gain[0]
    site_tensor = edge_site[0]
    mpo_terms = left_block.shape[0]
    states = left_block.shape[1]
    first_rows, first_whole = relax_block(left_block, right_block, psi_one[0], kept[0, 0])
    halfway = jnp.dot(
        left_block.reshape(mpo_terms * states, states),
        site_tensor,
        preferred_element_type=jnp.float32,
    )
    halfway = halfway.astype(jnp.bfloat16).reshape(mpo_terms, states, states)
    outgoing = jnp.einsum("ki,wkj->wij", site_tensor, halfway, preferred_element_type=jnp.float32)
    outgoing = (outgoing * gain_row[:, None, None]).astype(jnp.bfloat16)
    arrived = shifted(outgoing, "seg", 1)
    incoming = jnp.where(lax.axis_index("seg") == 0, left_block, arrived)
    site_left = (first_whole * states ** (-0.5)).astype(jnp.bfloat16)
    halfway = jnp.dot(
        right_block.reshape(mpo_terms * states, states),
        site_left.T,
        preferred_element_type=jnp.float32,
    )
    halfway = halfway.astype(jnp.bfloat16).reshape(mpo_terms, states, states)
    right_next = jnp.einsum("ik,wkj->wij", site_left, halfway, preferred_element_type=jnp.float32)
    right_next = (right_next * gain_row[:, None, None]).astype(jnp.bfloat16)
    second_rows, second_whole = relax_block(incoming, right_next, psi_two[0], kept[0, 1])
    return (first_rows[None], second_rows[None])


def solution(mesh):
    placed = (
        P("seg", "sec", None, None),
        P("seg", "sec", None, None),
        P("seg", None, None),
        P("seg", None, None),
        P("seg", None, None),
        P("seg", "sec"),
        P("seg", None),
    )
    return jax.shard_map(
        on_device,
        mesh=mesh,
        in_specs=placed,
        out_specs=(P("seg", "sec", None), P("seg", "sec", None)),
        check_vma=False,
    )
```

profile of v0, /device:TPU:1, one launch (start us, length us, event | category | flops | bytes accessed | tf_op | source)
XLA Modules:
  0.0 784.8 jit_solution(2778095177959367723)
XLA Ops:
  11.6 4.9 fusion
  16.5 5.6 copy.18
  22.1 3.6 fusion.30
  25.9 2.9 convolution_convert_fusion.4
  28.8 3.1 fusion.4
  31.9 5.6 collective-permute-start
  37.5 5.6 copy.21
  43.2 94.1 %all-reduce.7.cloned.1.call-done = bf16[256,256]{1,0:T(8,128)(2,1)} async-done(((bf16[256,256]{1,0:T(8,128)(2,1)}), bf16[256,256]{1,0:T(8,128)(2,1)}) %all-reduce.7.cloned.1.call-update) | async-done | bytes 131088 | tf_op jit(solution)/shard_map/psum | solution.py:46
  137.2 1.7 multiply_reduce_fusion.16
  140.2 1.7 multiply_reduce_fusion.15
  143.7 4.8 fusion.1
  148.5 5.6 copy.19
  154.1 3.6 fusion.27
  158.5 107.2 %all-reduce.9.cloned.1.call-done = bf16[256,256]{1,0:T(8,128)(2,1)} async-done(((bf16[256,256]{1,0:T(8,128)(2,1)}), bf16[256,256]{1,0:T(8,128)(2,1)}) %all-reduce.9.cloned.1.call-update) | async-done | bytes 131088 | tf_op jit(solution)/shard_map/psum | solution.py:46
  272.2 4.7 fusion.2
  276.9 5.6 copy.20
  282.5 3.6 fusion.24
  288.7 105.4 %all-reduce.11.cloned.1.call-done = bf16[256,256]{1,0:T(8,128)(2,1)} async-done(((bf16[256,256]{1,0:T(8,128)(2,1)}), bf16[256,256]{1,0:T(8,128)(2,1)}) %all-reduce.11.cloned.1.call-update) | async-done | bytes 131088 | tf_op jit(solution)/shard_map/psum | solution.py:46
  401.1 2.8 fusion.3
  403.9 5.6 copy.24
  409.5 5.1 fusion.5
  414.7 2.1 bitcast_select_fusion
  416.7 4.0 copy.23
  422.7 1.7 fusion.21
  424.5 109.8 %all-reduce.13.cloned.1.call-done = bf16[256,256]{1,0:T(8,128)(2,1)} async-done(((bf16[256,256]{1,0:T(8,128)(2,1)}), bf16[256,256]{1,0:T(8,128)(2,1)}) %all-reduce.13.cloned.1.call-update) | async-done | bytes 131088 | tf_op jit(solution)/shard_map/psum | solution.py:46
  534.3 1.7 multiply_reduce_fusion.7
  537.3 1.7 multiply_reduce_fusion.6
  542.8 1.7 fusion.22
  544.5 107.9 %all-reduce.15.cloned.1.call-done = bf16[256,256]{1,0:T(8,128)(2,1)} async-done(((bf16[256,256]{1,0:T(8,128)(2,1)}), bf16[256,256]{1,0:T(8,128)(2,1)}) %all-reduce.15.cloned.1.call-update) | async-done | bytes 131088 | tf_op jit(solution)/shard_map/psum | solution.py:46
  663.9 106.6 %all-reduce.17.cloned.1.call-done = bf16[256,256]{1,0:T(8,128)(2,1)} async-done(((bf16[256,256]{1,0:T(8,128)(2,1)}), bf16[256,256]{1,0:T(8,128)(2,1)}) %all-reduce.17.cloned.1.call-update) | async-done | bytes 131088 | tf_op jit(solution)/shard_map/psum | solution.py:46
  770.5 1.7 multiply_reduce_fusion.1
  773.6 2.3 multiply_reduce_fusion
  (65 shorter events, 32.8 us)
Async XLA Ops:
  7.2 15.0 %copy-start = (bf16[1,25,256,256]{3,2,1,0:T(8,128)(2,1)S(1)}, bf16[1,25,256,256]{3,2,1,0:T(8,128)(2,1)}, u32[]{:S(2)}) copy-start(bf16[1,25,256,256]{3,2,1,0:T(8,128)(2,1)} %param.8) | copy-start | bytes 9830404
  7.2 130.1 %all-reduce.7.cloned.1.call-start = ((), (), s32[]{:S(2)}) async-start(), calls=%async_computation | async-start | bytes 262144 | tf_op jit(solution)/shard_map/psum | solution.py:46
  22.1 3.7 copy-start.13
  25.8 3.0 copy-start.14
  25.8 239.9 %all-reduce.9.cloned.1.call-start = ((), (), s32[]{:S(2)}) async-start(), calls=%async_computation.1 | async-start | bytes 262144 | tf_op jit(solution)/shard_map/psum | solution.py:46
  31.9 382.8 %collective-permute-start = (bf16[25,256,256]{1,2,0:T(8,128)(2,1)}, bf16[25,256,256]{1,2,0:T(8,128)(2,1)}, u32[]{:S(2)}, u32[]{:S(2)}) collective-permute-start(bf16[25,256,256]{1,2,0:T(8,128)(2,1)} %fusion.4), channel_id=1, source_target_pairs={{0,16},{16,32},{32,48},{48,64},{64,80},{80,96},{96,112},{112,128},... | collective-permute-start | bytes 9830408 | tf_op jit(solution)/shard_map/ppermute | solution.py:16
  37.5 99.7 %copy-start.9 = (bf16[1,256,256]{2,1,0:T(8,128)(2,1)S(1)}, bf16[1,256,256]{2,1,0:T(8,128)(2,1)}, u32[]{:S(2)}) copy-start(bf16[1,256,256]{2,1,0:T(8,128)(2,1)} %param.10) | copy-start | bytes 393220
  143.7 125.0 %copy-start.3 = (f32[256,256]{1,0:T(8,128)}, f32[256,256]{1,0:T(8,128)S(1)}, u32[]{:S(2)}) copy-start(f32[256,256]{1,0:T(8,128)S(1)} %multiply_divide_fusion.4) | copy-start | bytes 786436
  157.8 236.3 %all-reduce.11.cloned.1.call-start = ((), (), s32[]{:S(2)}) async-start(), calls=%async_computation.2 | async-start | bytes 262144 | tf_op jit(solution)/shard_map/psum | solution.py:46
  286.1 248.2 %all-reduce.13.cloned.1.call-start = ((), (), s32[]{:S(2)}) async-start(), calls=%async_computation.3 | async-start | bytes 262144 | tf_op jit(solution)/shard_map/psum | solution.py:46
  400.4 0.7 copy-start.11
  403.9 5.6 copy-start.12
  409.5 5.2 copy-start.2
  416.7 4.1 copy-start.10
  420.8 1.9 copy-start.6
  424.4 228.0 %all-reduce.15.cloned.1.call-start = ((), (), s32[]{:S(2)}) async-start(), calls=%async_computation.4 | async-start | bytes 262144 | tf_op jit(solution)/shard_map/psum | solution.py:46
  540.9 1.9 copy-start.7
  544.5 226.0 %all-reduce.17.cloned.1.call-start = ((), (), s32[]{:S(2)}) async-start(), calls=%async_computation.5 | async-start | bytes 262144 | tf_op jit(solution)/shard_map/psum | solution.py:46
  658.8 1.0 copy-start.4
  658.8 2.0 copy-start.8
  659.9 118.1 %copy-start.1 = (bf16[1,25,256,256]{3,2,1,0:T(8,128)(2,1)S(1)}, bf16[1,25,256,256]{3,2,1,0:T(8,128)(2,1)}, u32[]{:S(2)}) copy-start(bf16[1,25,256,256]{3,2,1,0:T(8,128)(2,1)} %param.8) | copy-start | bytes 9830404
  660.8 109.6 %copy-start.5 = (f32[256,256]{1,0:T(8,128)S(1)}, f32[256,256]{1,0:T(8,128)}, u32[]{:S(2)}) copy-start(f32[256,256]{1,0:T(8,128)} %copy-done.4) | copy-start | bytes 786436
Sparse Core Ops, SparseCore 0:
  25.9 111.2 all-reduce.6
  157.9 107.7 all-reduce.8
  286.2 107.7 all-reduce.10
  424.6 109.6 all-reduce.12
  544.6 107.7 all-reduce.14
  662.7 107.7 all-reduce.16
where the time goes:
time: 787 us; the launch traced here: 785 us
  waiting for transfers between devices  631 us (80%)
  matrix products  47.2 us (6%)
  local copies, waits for them, and re-layouts  38.3 us (5%)
  other arithmetic  34.3 us (4%)
  between operations  27.8 us (4%)
    psum x6, waiting for transfers between devices, relax_block(): lax.psum(apply_block(left_block, right_block, vector.astype(jnp.bfloat16)...  631 us
    dot_general x6, matrix products, apply_block(): jnp.dot(left_block.reshape(mpo_terms * states, states), vector_bf, prefer...  17.4 us
    convert_element_type x3, local copies, waits for them, and re-layouts, apply_block(): partial_prod.astype(jnp.bfloat16).reshape(mpo_terms, states, states)  16.9 us
    dot_general x6, matrix products, apply_block(): lax.dot_general(partial_prod, right_block, (((0, 2), (0, 2)), ((), ())),...  15.9 us
  transfers between devices with their start and end apart: 7, of which 6 were waited for; matrix products, arithmetic and copies ran while one was open for 9% of the time, Pallas kernels for 0%

commit v1 on v0

v1 whole, which is shorter than its diff:
```python
import functools

import jax
import jax.numpy as jnp
from jax import lax
from jax.experimental import pallas as pl
from jax.experimental.pallas import tpu as pltpu
from jax.sharding import PartitionSpec as P

ITERS = 3
EPSILON = 1e-06
DESCENT = 0.3
CHUNK = 5
VMEM_LIMIT = 40 * 1024 * 1024

F32 = jnp.float32
BF16 = jnp.bfloat16


def dot(a, b, dims=((1,), (0,))):
    return lax.dot_general(a, b, (dims, ((), ())), preferred_element_type=F32)


def live_rows(shape, live):
    return lax.broadcasted_iota(jnp.int32, shape, 0) < live


def normalised(z, states):
    return z * (states / jnp.sqrt(jnp.sum(z * z) + EPSILON))


def stepped(vector, product, states):
    energy = jnp.sum(vector * product) / jnp.sum(vector * vector)
    return normalised(vector - DESCENT * (product - energy * vector), states)


def block_copies(left, right, left_buf, right_buf, sems):
    terms = left_buf.shape[0]
    chunk = CHUNK if terms % CHUNK == 0 else 1
    return chunk, [
        (
            pltpu.make_async_copy(left.at[0, pl.ds(n, chunk)], left_buf.at[pl.ds(n, chunk)], sems.at[0, n // chunk]),
            pltpu.make_async_copy(right.at[0, pl.ds(n, chunk)], right_buf.at[pl.ds(n, chunk)], sems.at[1, n // chunk]),
        )
        for n in range(0, terms, chunk)
    ]


def contract(vector, copies, chunk, left_buf, right_buf, acc, weight=None):
    states = vector.shape[0]
    for index, (left_copy, right_copy) in enumerate(copies):
        left_copy.wait()
        right_copy.wait()
        first = index * chunk
        terms = dot(left_buf[first : first + chunk].reshape(chunk * states, states), vector)
        total = None
        for n in range(chunk):
            term = terms[n * states : (n + 1) * states]
            if weight is not None:
                term = term * weight(first + n)
            part = dot(term.astype(BF16), right_buf[first + n])
            total = part if total is None else total + part
        if index == 0:
            acc[...] = total
        else:
            acc[...] += total


def hand_out(acc, mine, theirs):
    half = mine.shape[0]
    core = lax.rem(lax.axis_index("sec"), 2)
    mine[...] = acc[pl.ds(pl.multiple_of(core * half, half), half), :].astype(BF16)
    theirs[...] = acc[pl.ds(pl.multiple_of((1 - core) * half, half), half), :].astype(BF16)


def product_of(summed, live):
    states = summed.shape[2]
    product = summed[...].reshape(states, states).astype(F32)
    return jnp.where(live_rows(product.shape, live), product, 0.0)


def first_start(kept, start, left, right, vector, mine, theirs, left_buf, right_buf, acc, sems):
    chunk, copies = block_copies(left, right, left_buf, right_buf, sems)
    for pair in copies:
        pair[0].start()
        pair[1].start()
    states = start.shape[1]
    begun = jnp.where(live_rows((states, states), kept[0, 0]), start[0].astype(F32), 0.0)
    current = normalised(begun, states)
    vector[...] = current
    contract(current.astype(BF16), copies, chunk, left_buf, right_buf, acc)
    hand_out(acc, mine, theirs)


def first_step(kept, vector, summed, left, right, after, mine, theirs, left_buf, right_buf, acc, sems):
    chunk, copies = block_copies(left, right, left_buf, right_buf, sems)
    for pair in copies:
        pair[0].start()
        pair[1].start()
    states = vector.shape[1]
    current = stepped(vector[...], product_of(summed, kept[0, 0]), states)
    after[...] = current
    contract(current.astype(BF16), copies, chunk, left_buf, right_buf, acc)
    hand_out(acc, mine, theirs)


def second_blocks(left, arrived, right, left_buf, right_buf, sems):
    chunk, copies = block_copies(arrived, right, left_buf, right_buf, sems)
    at_start = lax.axis_index("seg") == 0

    @pl.when(at_start)
    def _():
        for index in range(len(copies)):
            part = pl.ds(index * chunk, chunk)
            pltpu.make_async_copy(left.at[0, part], left_buf.at[part], sems.at[0, index]).start()

    @pl.when(jnp.logical_not(at_start))
    def _():
        for left_copy, _ in copies:
            left_copy.start()

    for _, right_copy in copies:
        right_copy.start()
    return chunk, copies, at_start


def second_apply(current, site, edge, gain, gain_before, blocks, left_buf, right_buf, acc, mine, theirs):
    chunk, copies, at_start = blocks
    shape = edge.shape
    one = lax.broadcasted_iota(jnp.int32, shape, 0) == lax.broadcasted_iota(jnp.int32, shape, 1)
    edge = jnp.where(at_start, one.astype(F32), edge.astype(F32)).astype(BF16)
    inner = dot(current.astype(BF16), site).astype(BF16)
    inner = dot(edge, inner).astype(BF16)

    def weight(n):
        return gain[0, n] * jnp.where(at_start, 1.0, gain_before[0, n])

    contract(inner, copies, chunk, left_buf, right_buf, acc, weight)
    outer = dot(acc[...].astype(BF16), site, ((1,), (1,))).astype(BF16)
    acc[...] = dot(edge, outer, ((0,), (0,)))
    hand_out(acc, mine, theirs)


def second_start(
    kept, vector, summed, start, edge, gain, gain_before, left, arrived, right,
    rows, site, after, mine, theirs, left_buf, right_buf, acc, sems,
):
    blocks = second_blocks(left, arrived, right, left_buf, right_buf, sems)
    states = vector.shape[1]
    share = rows.shape[1]
    acc[...] = stepped(vector[...], product_of(summed, kept[0, 0]), states)
    rows[0] = acc[pl.ds(pl.multiple_of(lax.axis_index("sec") * share, share), share), :]
    site_left = (acc[...] * states**-0.5).astype(BF16)
    site[...] = site_left
    begun = jnp.where(live_rows((states, states), kept[0, 1]), start[0].astype(F32), 0.0)
    current = normalised(begun, states)
    after[...] = current
    second_apply(current, site_left, edge[0], gain, gain_before, blocks, left_buf, right_buf, acc, mine, theirs)


def second_step(
    kept, vector, summed, site, edge, gain, gain_before, left, arrived, right,
    after, mine, theirs, left_buf, right_buf, acc, sems,
):
    blocks = second_blocks(left, arrived, right, left_buf, right_buf, sems)
    states = vector.shape[1]
    current = stepped(vector[...], product_of(summed, kept[0, 1]), states)
    after[...] = current
    second_apply(current, site[...], edge[0], gain, gain_before, blocks, left_buf, right_buf, acc, mine, theirs)


def second_end(kept, vector, summed, rows, whole):
    states = vector.shape[1]
    share = rows.shape[1]
    whole[...] = stepped(vector[...], product_of(summed, kept[0, 1]), states)
    rows[0] = whole[pl.ds(pl.multiple_of(lax.axis_index("sec") * share, share), share), :]


def on_device(left_env, right_env, edge_site, psi_one, psi_two, mpo_gain, kept):
    terms, states = left_env.shape[1], left_env.shape[2]
    sections, segments = lax.axis_size("sec"), lax.axis_size("seg")
    chips, half, share = sections // 2, states // 2, states // sections
    pairs = [[2 * n, 2 * n + 1] for n in range(chips)]
    columns = [[2 * n + core for n in range(chips)] for core in range(2)]
    onward = [(n, n + 1) for n in range(segments - 1)]

    smem = pl.BlockSpec(memory_space=pltpu.SMEM)
    vmem = pl.BlockSpec(memory_space=pltpu.VMEM)
    hbm = pl.BlockSpec(memory_space=pl.ANY)
    block = jax.ShapeDtypeStruct((states, states), F32)
    site_block = jax.ShapeDtypeStruct((states, states), BF16)
    half_block = jax.ShapeDtypeStruct((half, states), BF16)
    rows_block = jax.ShapeDtypeStruct((1, share, states), F32)
    buffers = [
        pltpu.VMEM((terms, states, states), BF16),
        pltpu.VMEM((terms, states, states), BF16),
        pltpu.VMEM((states, states), F32),
        pltpu.SemaphoreType.DMA((2, terms // CHUNK if terms % CHUNK == 0 else terms)),
    ]
    params = pltpu.CompilerParams(vmem_limit_bytes=VMEM_LIMIT)
    cost = pl.CostEstimate(
        flops=4 * terms * states**3, bytes_accessed=4 * terms * states**2, transcendentals=0
    )

    def call(kernel, ins, outs, name, scratch=buffers, cost=cost):
        return pl.pallas_call(
            kernel,
            in_specs=ins,
            out_specs=[vmem] * len(outs),
            out_shape=outs,
            scratch_shapes=scratch,
            compiler_params=params,
            cost_estimate=cost,
            name=name,
        )

    def summed(mine, theirs):
        other = lax.ppermute(theirs, "sec", [(n, n ^ 1) for n in range(sections)])
        chip = (mine.astype(F32) + other.astype(F32)).astype(BF16)
        spread = jnp.broadcast_to(chip[None], (chips, half, states))
        parts = lax.all_to_all(spread, "sec", 0, 0, axis_index_groups=columns)
        total = jnp.sum(parts.astype(F32), axis=0).astype(BF16)
        return lax.all_gather(total, "sec", axis=0, axis_index_groups=pairs)

    arrived = lax.ppermute(left_env, "seg", onward)
    edge = lax.ppermute(edge_site, "seg", onward)
    gain_before = lax.ppermute(mpo_gain, "seg", onward)

    vector, mine, theirs = call(
        first_start, [smem, vmem, hbm, hbm], [block, half_block, half_block], "first_start"
    )(kept, psi_one, left_env, right_env)
    for _ in range(ITERS - 1):
        vector, mine, theirs = call(
            first_step, [smem, vmem, vmem, hbm, hbm], [block, half_block, half_block], "first_step"
        )(kept, vector, summed(mine, theirs), left_env, right_env)

    first_rows, site, vector, mine, theirs = call(
        second_start,
        [smem, vmem, vmem, vmem, vmem, smem, smem, hbm, hbm, hbm],
        [rows_block, site_block, block, half_block, half_block],
        "second_start",
    )(kept, vector, summed(mine, theirs), psi_two, edge, mpo_gain, gain_before, left_env, arrived, right_env)
    for _ in range(ITERS - 1):
        vector, mine, theirs = call(
            second_step,
            [smem, vmem, vmem, vmem, vmem, smem, smem, hbm, hbm, hbm],
            [block, half_block, half_block],
            "second_step",
        )(kept, vector, summed(mine, theirs), site, edge, mpo_gain, gain_before, left_env, arrived, right_env)
    (second_rows,) = call(
        second_end,
        [smem, vmem, vmem],
        [rows_block],
        "second_end",
        [pltpu.VMEM((states, states), F32)],
        None,
    )(kept, vector, summed(mine, theirs))
    return first_rows, second_rows


def solution(mesh):
    placed = (
        P("seg", "sec", None, None),
        P("seg", "sec", None, None),
        P("seg", None, None),
        P("seg", None, None),
        P("seg", None, None),
        P("seg", "sec"),
        P("seg", None),
    )
    return jax.shard_map(
        on_device,
        mesh=mesh,
        in_specs=placed,
        out_specs=(P("seg", "sec", None), P("seg", "sec", None)),
        check_vma=False,
    )
```

time: 787 us -> 230 us (0.29)
  waiting for transfers between devices: 631 us -> 30.4 us
  blocking collectives: 0 us -> 96.3 us
  matrix products: 47.2 us -> 0 us
  Pallas kernels: 0 us -> 40.9 us
  between operations: 27.8 us -> 0.87 us
  other arithmetic: 34.3 us -> 7.68 us
  starting transfers between devices: 6.06 us -> 26.7 us
  local copies, waits for them, and re-layouts: 38.3 us -> 25.9 us
    psum x6 -> x0, waiting for transfers between devices: 631 us -> none  [relax_block(): lax.psum(apply_block(left_block, right_block, vector.astype(jnp.bfloat16)...]
    all_to_all x0 -> x4, blocking collectives: none -> 83.6 us  [summed(): parts = lax.all_to_all(spread, 'sec', 0, 0, axis_index_groups=columns)]
    dot_general x16 -> x0, matrix products: 47.2 us -> none  [the longest x6 17.4 us: apply_block(): jnp.dot(left_block.reshape(mpo_terms * states, states), vector_bf, prefer...]
    pallas_call x0 -> x7, Pallas kernels: none -> 40.9 us  [the longest x2 13.7 us: on_device(): call(second_step, [smem, vmem, vmem, vmem, vmem, smem, smem, hbm, hbm, hb...]
    all_to_all x0 -> x2, waiting for transfers between devices: none -> 25 us  [summed(): parts = lax.all_to_all(spread, 'sec', 0, 0, axis_index_groups=columns)]
    convert_element_type x4 -> x0, local copies, waits for them, and re-layouts: 22.5 us -> none  [the longest x3 16.9 us: apply_block(): partial_prod.astype(jnp.bfloat16).reshape(mpo_terms, states, states)]
    reduce_sum x14 -> x6, other arithmetic: 24.1 us -> 7.57 us  [summed(): total = jnp.sum(parts.astype(F32), axis=0).astype(BF16)]
    unnamed x31 -> x46, local copies, waits for them, and re-layouts: 9.05 us -> 24.1 us
  transfers between devices with their start and end apart: 7 -> 11, of which waited for: 6 -> 8; matrix products, arithmetic and copies ran while one was open for 9% -> 2% of each run, Pallas kernels for 0% -> 5%
where the time goes in v1:
time: 230 us; the launch traced here: 229 us
  blocking collectives  96.3 us (42%)
  Pallas kernels  40.9 us (18%)
  waiting for transfers between devices  30.4 us (13%)
  starting transfers between devices  26.7 us (12%)
  local copies, waits for them, and re-layouts  25.9 us (11%)
  other arithmetic  7.68 us (3%)
    all_to_all x4, blocking collectives, summed(): parts = lax.all_to_all(spread, 'sec', 0, 0, axis_index_groups=columns)  83.6 us
    all_to_all x2, waiting for transfers between devices, summed(): parts = lax.all_to_all(spread, 'sec', 0, 0, axis_index_groups=columns)  25 us
    unnamed x46, local copies, waits for them, and re-layouts  24.1 us
    pallas_call x2, Pallas kernels, on_device(): call(second_step, [smem, vmem, vmem, vmem, vmem, smem, smem, hbm, hbm, hb...  13.7 us
    all_gather x6, blocking collectives, summed(): return lax.all_gather(total, 'sec', axis=0, axis_index_groups=pairs)  12.7 us
    pallas_call x2, Pallas kernels, on_device(): call(first_step, [smem, vmem, vmem, hbm, hbm], [block, half_block, half_b...  12.4 us
    all_to_all x2, starting transfers between devices, summed(): parts = lax.all_to_all(spread, 'sec', 0, 0, axis_index_groups=columns)  10.6 us
    reduce_sum x6, other arithmetic, summed(): total = jnp.sum(parts.astype(F32), axis=0).astype(BF16)  7.57 us
  transfers between devices with their start and end apart: 11, of which 8 were waited for; matrix products, arithmetic and copies ran while one was open for 2% of the time, Pallas kernels for 5%

profile of v1, /device:TPU:1, one launch (start us, length us, event | category | flops | bytes accessed | tf_op | source)
XLA Modules:
  0.0 228.8 jit_solution(12449056011258526194)
XLA Ops:
  0.6 1.9 copy-done
  2.6 1.9 copy-done.2
  6.0 6.0 %first_start.1 = (f32[256,256]{1,0:T(8,128)S(1)}, bf16[128,256]{1,0:T(8,128)(2,1)S(1)}, bf16[128,256]{1,0:T(8,128)(2,1)S(1)}) custom-call(s32[1,2]{1,0:T(1,128)S(1)} %copy-done.20, bf16[1,256,256]{2,1,0:T(8,128)(2,1)S(1)} %copy-done.19, bf16[1,25,256,256]{3,2,1,0:T(8,128)(2,1)S(1)} %copy-done, bf16[1,25,256,256]{3,2,1,0:T(8,128)(2,1)S(1)} %copy-done.2), custom_call_target="tpu_custom_call" | custom-call | flops 1677721600 | bytes 6553600 | tf_op jit(solution)/shard_map/first_start/pallas_call | solution.py:229
  12.0 3.3 %collective-permute-start = (bf16[128,256]{1,0:T(8,128)(2,1)S(1)}, bf16[128,256]{1,0:T(8,128)(2,1)S(1)}, u32[]{:S(2)}, u32[]{:S(2)}) collective-permute-start(bf16[128,256]{1,0:T(8,128)(2,1)S(1)} %get-tuple-element.24), channel_id=1, source_target_pairs={{0,1},{1,0},{2,3},{3,2},{4,5},{5,4},{6,7},{7,6},{8,9},{9,8},{10,11... | collective-permute-start | bytes 196616 | tf_op jit(solution)/shard_map/ppermute | solution.py:218
  17.1 6.4 %all-to-all-start = ((bf16[8,128,256]{2,1,0:T(8,128)(2,1)}), bf16[8,128,256]{2,1,0:T(8,128)(2,1)}, u32[]{:S(2)}, u32[]{:S(2)}) async-start(bf16[8,128,256]{2,1,0:T(8,128)(2,1)} %broadcast_in_dim.12), calls=%async_computation | async-start | bytes 1048576 | tf_op jit(solution)/shard_map/all_to_all | solution.py:221
  23.5 4.8 %collective-permute-start.5 = (bf16[1,25,256,256]{3,2,1,0:T(8,128)(2,1)S(1)}, bf16[1,25,256,256]{3,2,1,0:T(8,128)(2,1)}, u32[]{:S(2)}, u32[]{:S(2)}) collective-permute-start(bf16[1,25,256,256]{3,2,1,0:T(8,128)(2,1)S(1)} %copy-done.1), channel_id=1, source_target_pairs={{0,16},{16,32},{32,48},{48,64},{64,80},{80,96},{96,112},{112,128},... | collective-permute-start | bytes 9830408 | tf_op jit(solution)/shard_map/ppermute | solution.py:225
  28.3 13.3 %all-to-all-done = bf16[8,128,256]{2,1,0:T(8,128)(2,1)} async-done(((bf16[8,128,256]{2,1,0:T(8,128)(2,1)}), bf16[8,128,256]{2,1,0:T(8,128)(2,1)}, u32[]{:S(2)}, u32[]{:S(2)}) %all-to-all-start) | async-done | bytes 524320 | tf_op jit(solution)/shard_map/all_to_all | solution.py:221
  41.6 1.8 reduce_sum.72
  43.4 2.2 all-gather
  45.6 1.9 copy-done.3
  47.5 6.2 %first_step.2 = (f32[256,256]{1,0:T(8,128)S(1)}, bf16[128,256]{1,0:T(8,128)(2,1)S(1)}, bf16[128,256]{1,0:T(8,128)(2,1)S(1)}) custom-call(s32[1,2]{1,0:T(1,128)S(1)} %copy-done.21, f32[256,256]{1,0:T(8,128)S(1)} %get-tuple-element.22.vector, bf16[2,128,256]{2,1,0:T(8,128)(2,1)S(1)} %bitcast.9, bf16[1,25,256,256]{3,2,1,0:T(8,128)(2,1)S(1)} %copy-done.1, ...), custom_call_target="tpu_custom_call" | custom-call | flops 1677721600 | bytes 6553600 | tf_op jit(solution)/shard_map/first_step/pallas_call | solution.py:233
  55.7 21.1 %all_to_all.30 = bf16[8,128,256]{2,1,0:T(8,128)(2,1)} all-to-all(bf16[8,128,256]{2,1,0:T(8,128)(2,1)S(1)} %broadcast_in_dim.13), channel_id=1, replica_groups={{0,2,4,6,8,10,12,14},{1,3,5,7,9,11,13,15},{16,18,20,22,24,26,28,30},{17..., dimensions={0} | all-to-all | bytes 1048576 | tf_op jit(solution)/shard_map/all_to_all | solution.py:221
  77.9 2.0 all-gather.1
  80.0 1.9 copy-done.4
  82.8 6.2 %first_step.3 = (f32[256,256]{1,0:T(8,128)S(1)}, bf16[128,256]{1,0:T(8,128)(2,1)S(1)}, bf16[128,256]{1,0:T(8,128)(2,1)S(1)}) custom-call(s32[1,2]{1,0:T(1,128)S(1)} %copy-done.21, f32[256,256]{1,0:T(8,128)S(1)} %copy-done.15, bf16[2,128,256]{2,1,0:T(8,128)(2,1)S(1)} %bitcast.10, bf16[1,25,256,256]{3,2,1,0:T(8,128)(2,1)S(1)} %copy-done.1, ...), custom_call_target="tpu_custom_call" | custom-call | flops 1677721600 | bytes 6553600 | tf_op jit(solution)/shard_map/first_step/pallas_call | solution.py:233
  91.8 4.2 %all-to-all-start.2 = ((bf16[8,128,256]{2,1,0:T(8,128)(2,1)}), bf16[8,128,256]{2,1,0:T(8,128)(2,1)}, u32[]{:S(2)}, u32[]{:S(2)}) async-start(bf16[8,128,256]{2,1,0:T(8,128)(2,1)} %broadcast_in_dim.14), calls=%async_computation.2 | async-start | bytes 1048576 | tf_op jit(solution)/shard_map/all_to_all | solution.py:221
  96.0 3.1 %collective-permute-start.3 = (bf16[1,256,256]{2,1,0:T(8,128)(2,1)}, bf16[1,256,256]{2,1,0:T(8,128)(2,1)S(1)}, u32[]{:S(2)}, u32[]{:S(2)}) collective-permute-start(bf16[1,256,256]{2,1,0:T(8,128)(2,1)} %param.9), channel_id=1, source_target_pairs={{0,16},{16,32},{32,48},{48,64},{64,80},{80,96},{96,112},{112,128},... | collective-permute-start | bytes 393224 | tf_op jit(solution)/shard_map/ppermute | solution.py:226
  99.1 3.1 %collective-permute-start.4 = (f32[1,25]{1,0:T(1,128)S(1)}, f32[1,25]{1,0:T(1,128)S(1)}, u32[]{:S(2)}, u32[]{:S(2)}) collective-permute-start(f32[1,25]{1,0:T(1,128)S(1)} %copy-done.22), channel_id=1, source_target_pairs={{0,16},{16,32},{32,48},{48,64},{64,80},{80,96},{96,112},{112,128},... | collective-permute-start | bytes 308 | tf_op jit(solution)/shard_map/ppermute | solution.py:227
  102.3 11.8 %all-to-all-done.2 = bf16[8,128,256]{2,1,0:T(8,128)(2,1)} async-done(((bf16[8,128,256]{2,1,0:T(8,128)(2,1)}), bf16[8,128,256]{2,1,0:T(8,128)(2,1)}, u32[]{:S(2)}, u32[]{:S(2)}) %all-to-all-start.2) | async-done | bytes 524320 | tf_op jit(solution)/shard_map/all_to_all | solution.py:221
  115.1 2.0 all-gather.2
  117.2 1.9 copy-done.5
  121.0 7.1 %second_start.1 = (f32[1,16,256]{2,1,0:T(8,128)}, bf16[256,256]{1,0:T(8,128)(2,1)S(1)}, f32[256,256]{1,0:T(8,128)S(1)}, bf16[128,256]{1,0:T(8,128)(2,1)S(1)}, bf16[128,256]{1,0:T(8,128)(2,1)S(1)}) custom-call(s32[1,2]{1,0:T(1,128)S(1)} %copy-done.21, f32[256,256]{1,0:T(8,128)S(1)} %copy-done.9, bf16[2,128,256]{2,1,0:T(8,128)(2,1)S(1)} %bitcast.6, ...), custom_call_target="tpu_custom_call" | custom-call | flops 1677721600 | bytes 6553600 | tf_op jit(solution)/shard_map/second_start/pallas_call | solution.py:237
  130.1 21.1 %all_to_all.31 = bf16[8,128,256]{2,1,0:T(8,128)(2,1)} all-to-all(bf16[8,128,256]{2,1,0:T(8,128)(2,1)S(1)} %broadcast_in_dim.15), channel_id=1, replica_groups={{0,2,4,6,8,10,12,14},{1,3,5,7,9,11,13,15},{16,18,20,22,24,26,28,30},{17..., dimensions={0} | all-to-all | bytes 1048576 | tf_op jit(solution)/shard_map/all_to_all | solution.py:221
  152.9 2.2 all-gather.3
  155.2 1.9 copy-done.6
  158.0 6.9 %second_step.2 = (f32[256,256]{1,0:T(8,128)S(1)}, bf16[128,256]{1,0:T(8,128)(2,1)S(1)}, bf16[128,256]{1,0:T(8,128)(2,1)S(1)}) custom-call(s32[1,2]{1,0:T(1,128)S(1)} %copy-done.21, f32[256,256]{1,0:T(8,128)S(1)} %copy-done.13, bf16[2,128,256]{2,1,0:T(8,128)(2,1)S(1)} %bitcast.8, bf16[256,256]{1,0:T(8,128)(2,1)S(1)} %get-tuple-element.35.site, ...), custom_call_target="tpu_custom_call" | custom-call | flops 1677721600 | bytes 6553600 | tf_op jit(solution)/shard_map/second_step/pallas_call | solution.py:244
  166.9 21.1 %all_to_all.32 = bf16[8,128,256]{2,1,0:T(8,128)(2,1)} all-to-all(bf16[8,128,256]{2,1,0:T(8,128)(2,1)S(1)} %broadcast_in_dim.16), channel_id=1, replica_groups={{0,2,4,6,8,10,12,14},{1,3,5,7,9,11,13,15},{16,18,20,22,24,26,28,30},{17..., dimensions={0} | all-to-all | bytes 1048576 | tf_op jit(solution)/shard_map/all_to_all | solution.py:221
  189.7 2.2 all-gather.4
  191.9 1.9 copy-done.7
  194.8 6.9 %second_step.3 = (f32[256,256]{1,0:T(8,128)S(1)}, bf16[128,256]{1,0:T(8,128)(2,1)S(1)}, bf16[128,256]{1,0:T(8,128)(2,1)S(1)}) custom-call(s32[1,2]{1,0:T(1,128)S(1)} %copy-done.21, f32[256,256]{1,0:T(8,128)S(1)} %copy-done.11, bf16[2,128,256]{2,1,0:T(8,128)(2,1)S(1)} %bitcast.7, bf16[256,256]{1,0:T(8,128)(2,1)S(1)} %get-tuple-element.35.site, ...), custom_call_target="tpu_custom_call" | custom-call | flops 1677721600 | bytes 6553600 | tf_op jit(solution)/shard_map/second_step/pallas_call | solution.py:244
  203.7 20.4 %all_to_all.33 = bf16[8,128,256]{2,1,0:T(8,128)(2,1)S(1)} all-to-all(bf16[8,128,256]{2,1,0:T(8,128)(2,1)S(1)} %broadcast_in_dim.17), channel_id=1, replica_groups={{0,2,4,6,8,10,12,14},{1,3,5,7,9,11,13,15},{16,18,20,22,24,26,28,30},{17..., dimensions={0} | all-to-all | bytes 1048576 | tf_op jit(solution)/shard_map/all_to_all | solution.py:221
  224.2 2.0 all-gather.5
  (71 shorter events, 27.3 us)
Async XLA Ops:
  0.6 1.9 copy-start
  2.6 1.9 copy-start.2
  4.5 0.9 copy-start.19
  6.0 17.5 %copy-start.1 = (bf16[1,25,256,256]{3,2,1,0:T(8,128)(2,1)S(1)}, bf16[1,25,256,256]{3,2,1,0:T(8,128)(2,1)}, u32[]{:S(2)}) copy-start(bf16[1,25,256,256]{3,2,1,0:T(8,128)(2,1)} %left.11) | copy-start | bytes 9830404
  6.0 39.6 %copy-start.21 = (s32[1,2]{1,0:T(1,128)S(1)}, s32[1,2]{1,0:T(1,128)}, u32[]{:S(2)}) copy-start(s32[1,2]{1,0:T(1,128)} %kept.13) | copy-start | bytes 28
  12.0 4.2 %collective-permute-start = (bf16[128,256]{1,0:T(8,128)(2,1)S(1)}, bf16[128,256]{1,0:T(8,128)(2,1)S(1)}, u32[]{:S(2)}, u32[]{:S(2)}) collective-permute-start(bf16[128,256]{1,0:T(8,128)(2,1)S(1)} %get-tuple-element.24), channel_id=1, source_target_pairs={{0,1},{1,0},{2,3},{3,2},{4,5},{5,4},{6,7},{7,6},{8,9},{9,8},{10,11... | collective-permute-start | bytes 196616 | tf_op jit(solution)/shard_map/ppermute | solution.py:218
  17.1 24.5 %all-to-all-start = ((bf16[8,128,256]{2,1,0:T(8,128)(2,1)}), bf16[8,128,256]{2,1,0:T(8,128)(2,1)}, u32[]{:S(2)}, u32[]{:S(2)}) async-start(bf16[8,128,256]{2,1,0:T(8,128)(2,1)} %broadcast_in_dim.12), calls=%async_computation | async-start | bytes 1048576 | tf_op jit(solution)/shard_map/all_to_all | solution.py:221
  23.5 93.6 %collective-permute-start.5 = (bf16[1,25,256,256]{3,2,1,0:T(8,128)(2,1)S(1)}, bf16[1,25,256,256]{3,2,1,0:T(8,128)(2,1)}, u32[]{:S(2)}, u32[]{:S(2)}) collective-permute-start(bf16[1,25,256,256]{3,2,1,0:T(8,128)(2,1)S(1)} %copy-done.1), channel_id=1, source_target_pairs={{0,16},{16,32},{32,48},{48,64},{64,80},{80,96},{96,112},{112,128},... | collective-permute-start | bytes 9830408 | tf_op jit(solution)/shard_map/ppermute | solution.py:225
  45.6 1.9 copy-start.3
  53.7 0.7 copy-start.14
  54.4 1.3 collective-permute-start.1
  80.0 1.9 copy-start.4
  81.9 0.9 copy-start.15
  82.8 16.3 %copy-start.22 = (f32[1,25]{1,0:T(1,128)S(1)}, f32[1,25]{1,0:T(1,128)}, u32[]{:S(2)}) copy-start(f32[1,25]{1,0:T(1,128)} %gain.5) | copy-start | bytes 304
  89.0 0.7 copy-start.8
  89.7 1.3 collective-permute-start.2
  91.8 22.2 %all-to-all-start.2 = ((bf16[8,128,256]{2,1,0:T(8,128)(2,1)}), bf16[8,128,256]{2,1,0:T(8,128)(2,1)}, u32[]{:S(2)}, u32[]{:S(2)}) async-start(bf16[8,128,256]{2,1,0:T(8,128)(2,1)} %broadcast_in_dim.14), calls=%async_computation.2 | async-start | bytes 1048576 | tf_op jit(solution)/shard_map/all_to_all | solution.py:221
  96.0 21.2 %collective-permute-start.3 = (bf16[1,256,256]{2,1,0:T(8,128)(2,1)}, bf16[1,256,256]{2,1,0:T(8,128)(2,1)S(1)}, u32[]{:S(2)}, u32[]{:S(2)}) collective-permute-start(bf16[1,256,256]{2,1,0:T(8,128)(2,1)} %param.9), channel_id=1, source_target_pairs={{0,16},{16,32},{32,48},{48,64},{64,80},{80,96},{96,112},{112,128},... | collective-permute-start | bytes 393224 | tf_op jit(solution)/shard_map/ppermute | solution.py:226
  99.1 18.0 %collective-permute-start.4 = (f32[1,25]{1,0:T(1,128)S(1)}, f32[1,25]{1,0:T(1,128)S(1)}, u32[]{:S(2)}, u32[]{:S(2)}) collective-permute-start(f32[1,25]{1,0:T(1,128)S(1)} %copy-done.22), channel_id=1, source_target_pairs={{0,16},{16,32},{32,48},{48,64},{64,80},{80,96},{96,112},{112,128},... | collective-permute-start | bytes 308 | tf_op jit(solution)/shard_map/ppermute | solution.py:227
  117.2 1.9 copy-start.5
  119.1 0.9 copy-start.9
  120.1 0.9 copy-start.18
  128.8 1.3 collective-permute-start.6
  155.2 1.9 copy-start.6
  157.1 0.9 copy-start.13
  164.9 0.7 copy-start.10
  165.6 1.3 collective-permute-start.7
  191.9 1.9 copy-start.7
  193.9 0.9 copy-start.11
  201.7 0.7 copy-start.16
  202.4 1.3 collective-permute-start.8
  226.2 0.9 copy-start.17
  (2 other events, 1.3 us)
